TPU v7x, 32 devices: a whole 2x2x4 slice. The times are simulated.
32 devices in a mesh: grp: 2 (over x), ep: 16 (over z, y, core).
Axes of the slice: x: 2, y: 2, z: 4, core: 2. Of those that a mesh axis runs over, the one named last changes fastest.
Arguments:
- states: bfloat16 [2, 1280, 2048], P(None, ('grp', 'ep')), may hold values from -6 to 6
- route_ids: int32 [2, 1280, 8], P(None, ('grp', 'ep')), may hold values from 0 to 15, all different within a row; in each aligned block of 40 rows (0 to 39, 40 to 79, ..., all dimensions but the last counted through in order) at most 30 rows name the same one
- route_gates: float32 [2, 1280, 8], P(None, ('grp', 'ep')), may hold values from 0.02 to 0.3
- moe_gain: float32 [2048], replicated, may hold values from 0.25 to 1.75
- final_gain: float32 [2048], replicated, may hold values from 0.25 to 1.75
- gate_proj: bfloat16 [16, 2048, 512], P('ep', 'grp'), may hold values from -0.125 to 0.125
- up_proj: bfloat16 [16, 2048, 512], P('ep', 'grp'), may hold values from -0.125 to 0.125
- down_proj: bfloat16 [16, 512, 2048], P('ep', 'grp'), may hold values from -0.25 to 0.25
- old_slots: int32 [16], replicated, may hold values from 0 to 15, each once
- new_slots: int32 [16], replicated, may hold values from 0 to 15, each once
- req_lengths: int32 [2, 2, 4], P(None, 'grp'), may hold values from 1 to 320, 640 in all within a row
- head_proj: bfloat16 [2048, 49152], P(None, ('grp', 'ep')), may hold values from -14 to 14
Outputs:
- mixed: bfloat16 [2, 1280, 2048], P(None, ('grp', 'ep'))
- moved_gate: bfloat16 [16, 2048, 512], P('ep', 'grp')
- moved_up: bfloat16 [16, 2048, 512], P('ep', 'grp')
- moved_down: bfloat16 [16, 512, 2048], P('ep', 'grp')
- log_probs: float32 [2, 8, 49152], P(None, None, ('grp', 'ep'))
Inputs may be any that keep to these rules, and one draw needn't show every extreme that they name: `route_ids`: in each aligned block of 40 rows (the rows of one device in one batch) no expert is named by more than 30 rows, a bound that some block reaches; the 8 ids of a row differ. `old_slots`: each expert once. `new_slots`: each expert once. `req_lengths`: the 4 lengths of a group in a batch sum to 640, and the largest is 320.
All inputs are finite; a program needn't handle non-finite values.
Results may differ from a plain program's by a relative error of at most 0.0035.
Values may be sent and summed in bfloat16 or wider, within the bound.
A program may use at most 128 MiB of HBM per device.

v0:
```python
import jax
import jax.numpy as jnp
from jax import lax
from jax.sharding import PartitionSpec as P


def normalize(rows, gain):
    scale = lax.rsqrt(jnp.mean(rows * rows, axis=-1, keepdims=True) + 1e-06)
    return (rows * scale * gain).astype(jnp.bfloat16)


def owner_table(placement):
    ident = jnp.arange(placement.shape[0], dtype=jnp.int32)
    hits = placement[None, :] == ident[:, None]
    return jnp.sum(jnp.where(hits, ident[None, :], 0), axis=1)


def exchange(value, axis, bit):
    n = lax.axis_size(axis)
    return lax.ppermute(value, axis, [(i, i ^ bit) for i in range(n)])


def relocate(weights, source):
    n = source.shape[0]
    rows = weights.reshape(n, weights.shape[1] // n, weights.shape[2])
    spread = lax.all_to_all(rows, "ep", split_axis=0, concat_axis=0, tiled=True)
    ordered = jnp.take(spread, source, axis=0)
    moved = lax.all_to_all(ordered, "ep", split_axis=0, concat_axis=0, tiled=True)
    return moved.reshape(weights.shape)


def split_bf16(value):
    high = lax.reduce_precision(value, 8, 7)
    middle = lax.reduce_precision(value - high, 8, 7)
    low = value - high - middle
    return [part.astype(jnp.bfloat16) for part in (high, middle, low)]


def scatter_sum(terms):
    n = lax.axis_size("ep")
    me = lax.axis_index("ep")
    bit = 1
    held = terms
    while bit < n:
        pairs = held.reshape(held.shape[0] // 2, 2, *held.shape[1:])
        mine = me // bit % 2
        sent = lax.dynamic_index_in_dim(pairs, 1 - mine, 1, keepdims=False)
        kept = lax.dynamic_index_in_dim(pairs, mine, 1, keepdims=False)
        held = kept + exchange(sent.astype(jnp.bfloat16), "ep", bit).astype(jnp.float32)
        bit *= 2
    return held[0]


def butterfly(value, axis, join):
    bit = 1
    while bit < lax.axis_size(axis):
        value = join(value, exchange(value, axis, bit))
        bit *= 2
    return value


def join_stats(ours, theirs):
    top = jnp.maximum(ours[0], theirs[0])
    total = ours[1] * jnp.exp(ours[0] - top) + theirs[1] * jnp.exp(theirs[0] - top)
    return jnp.stack([top, total])


def per_device(
    states,
    route_ids,
    route_gates,
    moe_gain,
    final_gain,
    gate_proj,
    up_proj,
    down_proj,
    old_slots,
    new_slots,
    req_lengths,
    head_proj,
):
    n_ep = lax.axis_size("ep")
    n_grp = lax.axis_size("grp")
    column = lax.axis_index("ep")
    group = lax.axis_index("grp")
    batches, tok_rows, width = states.shape
    n_slots = old_slots.shape[0]
    old_owner = owner_table(old_slots)
    source = jnp.take(old_owner, new_slots)
    residual = states.astype(jnp.float32)
    normed = normalize(residual, moe_gain).reshape(-1, width)
    chosen = route_ids[..., None] == old_slots
    slot_gates = jnp.sum(jnp.where(chosen, route_gates[..., None], 0.0), axis=2)
    parts = split_bf16(slot_gates.reshape(-1, n_slots))
    extra = -(-len(parts) * n_slots // 128) * 128
    coded = jnp.pad(jnp.concatenate(parts, axis=1), ((0, 0), (0, extra - len(parts) * n_slots)))
    rows = lax.all_gather(jnp.concatenate([normed, coded], axis=1), "ep", axis=0, tiled=True)
    gate_full = lax.all_gather(gate_proj[0], "grp", axis=0, tiled=True)
    up_full = lax.all_gather(up_proj[0], "grp", axis=0, tiled=True)
    down_full = lax.all_gather(down_proj[0], "grp", axis=0, tiled=True)
    tokens = rows[:, :width]
    codes = rows[:, width : width + len(parts) * n_slots].astype(jnp.float32)
    codes = codes.reshape(-1, len(parts), n_slots)
    own = jnp.arange(n_slots, dtype=jnp.int32) == column
    weight = jnp.sum(jnp.where(own, codes, 0.0), axis=(1, 2))
    gate_vals = jnp.dot(tokens, gate_full, preferred_element_type=jnp.float32)
    up_vals = jnp.dot(tokens, up_full, preferred_element_type=jnp.float32)
    hidden = (jax.nn.silu(gate_vals) * up_vals).astype(jnp.bfloat16)
    outputs = jnp.dot(hidden, down_full, preferred_element_type=jnp.float32)
    terms = (outputs * weight[:, None]).reshape(n_ep, -1, width)
    summed = scatter_sum(terms).reshape(states.shape)
    mixed = (residual + summed).astype(jnp.bfloat16)
    moved = tuple((relocate(weights, source) for weights in (gate_proj, up_proj, down_proj)))
    request_ends = jnp.cumsum(req_lengths[:, 0, :], axis=-1) - 1
    local_ends = request_ends - column * tok_rows
    picker = (
        local_ends[:, :, None] == jnp.arange(tok_rows, dtype=jnp.int32)[None, None, :]
    ).astype(jnp.bfloat16)
    tails = jnp.einsum("brt,btd->brd", picker, mixed, preferred_element_type=jnp.float32).astype(
        jnp.bfloat16
    )
    add = lambda a, b: a + b
    tails = butterfly(tails, "ep", add)
    here = (jnp.arange(n_grp, dtype=jnp.int32) == group)[None, :, None, None]
    spread = jnp.where(here, tails[:, None], jnp.zeros((), jnp.bfloat16))
    spread = butterfly(spread, "grp", add)
    finals = normalize(spread.reshape(-1, width).astype(jnp.float32), final_gain)
    logits = jnp.dot(finals, head_proj, preferred_element_type=jnp.float32)
    top = jnp.max(logits, axis=1)
    total = jnp.sum(jnp.exp(logits - top[:, None]), axis=1)
    stats = jnp.stack([top, total])
    stats = butterfly(stats, "ep", join_stats)
    stats = butterfly(stats, "grp", join_stats)
    log_probs = (logits - stats[0][:, None] - jnp.log(stats[1])[:, None]).reshape(
        batches, -1, logits.shape[1]
    )
    return (mixed, *moved, log_probs)


def solution(mesh):
    placed = (
        P(None, ("grp", "ep"), None),
        P(None, ("grp", "ep"), None),
        P(None, ("grp", "ep"), None),
        P(),
        P(),
        P("ep", "grp", None),
        P("ep", "grp", None),
        P("ep", "grp", None),
        P(),
        P(),
        P(None, "grp", None),
        P(None, ("grp", "ep")),
    )
    return jax.shard_map(
        per_device,
        mesh=mesh,
        in_specs=placed,
        out_specs=(
            P(None, ("grp", "ep"), None),
            P("ep", "grp", None),
            P("ep", "grp", None),
            P("ep", "grp", None),
            P(None, None, ("grp", "ep")),
        ),
        check_vma=False,
    )
```

profile of v0, /device:TPU:0, one launch (start us, length us, event | category | flops | bytes accessed | tf_op | source)
XLA Modules:
  0.0 420.9 jit_solution(121535099977191811)
XLA Ops:
  8.2 1.1 fusion.20
  9.4 1.1 fusion.22
  13.5 58.4 %all-gather.8.cloned.1.call-done = bf16[1280,2176]{1,0:T(8,128)(2,1)} async-done(((bf16[80,2176]{1,0:T(8,128)(2,1)}), bf16[1280,2176]{1,0:T(8,128)(2,1)}) %all-gather.8.cloned.1.call-update) | async-done | bytes 5570576 | tf_op jit(solution)/shard_map/all_gather | solution.py:97
  71.9 1.2 select_reduce_fusion
  73.1 32.1 %all-gather.10.cloned.1.call-done = bf16[1,2048,512]{2,1,0:T(8,128)(2,1)} async-done(((bf16[1,1024,512]{2,1,0:T(8,128)(2,1)}), bf16[1,2048,512]{2,1,0:T(8,128)(2,1)}) %all-gather.10.cloned.1.call-update) | async-done | bytes 2097168 | tf_op jit(solution)/shard_map/all_gather | solution.py:98
  105.2 5.4 %fusion.2 = f32[1280,512]{1,0:T(8,128)S(1)} fusion(bf16[1280,2176]{1,0:T(8,128)(2,1)} %all-gather.8.cloned.1.call-done, bf16[1,2048,512]{2,1,0:T(8,128)(2,1)} %all-gather.10.cloned.1.call-done), kind=kOutput, calls=%fused_computation.9 | convolution fusion | flops 2684354560 | bytes 9961472 | tf_op jit(solution)/shard_map/dot_general | solution.py:106
  110.6 29.3 %all-gather.14.cloned.1.call-done = bf16[1,512,2048]{2,1,0:T(8,128)(2,1)} async-done(((bf16[1,256,2048]{2,1,0:T(8,128)(2,1)}), bf16[1,512,2048]{2,1,0:T(8,128)(2,1)}) %all-gather.14.cloned.1.call-update) | async-done | bytes 2097168 | tf_op jit(solution)/shard_map/all_gather | solution.py:100
  139.9 34.6 %all-gather.12.cloned.1.call-done = bf16[1,2048,512]{2,1,0:T(8,128)(2,1)} async-done(((bf16[1,1024,512]{2,1,0:T(8,128)(2,1)}), bf16[1,2048,512]{2,1,0:T(8,128)(2,1)}) %all-gather.12.cloned.1.call-update) | async-done | bytes 2097168 | tf_op jit(solution)/shard_map/all_gather | solution.py:99
  174.5 11.4 %convolution_multiply_fusion = f32[1280,2048]{1,0:T(8,128)} fusion(f32[1280]{0:T(1024)S(1)} %select_reduce_fusion, bf16[1,512,2048]{2,1,0:T(8,128)(2,1)} %all-gather.14.cloned.1.call-done, bf16[1280,2176]{1,0:T(8,128)(2,1)} %all-gather.8.cloned.1.call-done, f32[1280,512]{1,0:T(8,128)S(1)} %fusion.2, bf16[1,2048,512]{2,1,0:T(8,128)(2,1)} %all-gather.12.cloned.1.call-done), kind=kOutput, calls=%fused_computation.4 | convolution fusion | flops 5375262720 | bytes 22549504 | tf_op jit(solution)/shard_map/dot_general | solution.py:109
  185.9 4.5 %fusion.10 = bf16[8,80,2048]{2,1,0:T(8,128)(2,1)} fusion(f32[8,2,80,2048]{3,2,1,0:T(8,128)} %bitcast.149, s32[]{:T(128)S(6)} %select_n.112), kind=kLoop, calls=%fused_computation.13 | loop fusion | bytes 5242884 | tf_op jit(solution)/shard_map/convert_element_type | solution.py:49
  190.3 30.5 %all_to_all.30 = bf16[16,64,512]{2,1,0:T(8,128)(2,1)} all-to-all(bf16[16,64,512]{2,1,0:T(8,128)(2,1)S(1)} %bitcast.151), channel_id=1, replica_groups=mesh['grp'=2,'ep'=16] {'ep'}, dimensions={0} | all-to-all | bytes 2097152 | tf_op jit(solution)/shard_map/all_to_all | solution.py:26
  220.8 5.0 %all-to-all-start = ((bf16[16,64,512]{2,1,0:T(8,128)(2,1)}), bf16[16,64,512]{2,1,0:T(8,128)(2,1)S(1)}, u32[]{:S(2)}, u32[]{:S(2)}) async-start(bf16[16,64,512]{2,1,0:T(8,128)(2,1)} %bitcast.14), calls=%async_computation | async-start | bytes 2097152 | tf_op jit(solution)/shard_map/all_to_all | solution.py:26
  225.9 4.1 bitcast_add_fusion
  230.0 2.3 copy-done
  232.5 1.9 collective-permute-start.1
  234.5 14.4 %all-to-all-done = bf16[16,64,512]{2,1,0:T(8,128)(2,1)S(1)} async-done(((bf16[16,64,512]{2,1,0:T(8,128)(2,1)}), bf16[16,64,512]{2,1,0:T(8,128)(2,1)S(1)}, u32[]{:S(2)}, u32[]{:S(2)}) %all-to-all-start) | async-done | bytes 1048608 | tf_op jit(solution)/shard_map/all_to_all | solution.py:26
  248.8 7.0 %all-to-all-start.4 = ((bf16[16,16,2048]{2,1,0:T(8,128)(2,1)}), bf16[16,16,2048]{2,1,0:T(8,128)(2,1)}, u32[]{:S(2)}, u32[]{:S(2)}) async-start(bf16[16,16,2048]{2,1,0:T(8,128)(2,1)} %bitcast.18), calls=%async_computation.4 | async-start | bytes 2097152 | tf_op jit(solution)/shard_map/all_to_all | solution.py:26
  256.7 19.4 %collective-permute-done.1 = bf16[4,80,2048]{2,1,0:T(8,128)(2,1)} collective-permute-done((bf16[4,80,2048]{2,1,0:T(8,128)(2,1)S(1)}, bf16[4,80,2048]{2,1,0:T(8,128)(2,1)}, u32[]{:S(2)}, u32[]{:S(2)}) %collective-permute-start.1) | collective-permute-done | bytes 1310752 | tf_op jit(solution)/shard_map/ppermute | solution.py:20
  276.1 2.4 bitcast_add_fusion.1
  279.5 3.7 collective-permute-start.2
  283.1 2.8 gather_fusion.3
  286.0 2.8 gather_fusion.2
  288.8 3.1 broadcast_select_fusion
  291.9 5.1 %all-to-all-start.1 = ((bf16[16,64,512]{2,1,0:T(8,128)(2,1)}), bf16[16,64,512]{2,1,0:T(8,128)(2,1)}, u32[]{:S(2)}, u32[]{:S(2)}) async-start(bf16[16,64,512]{2,1,0:T(8,128)(2,1)} %get-tuple-element.22), calls=%async_computation.1 | async-start | bytes 2097152 | tf_op jit(solution)/shard_map/all_to_all | solution.py:28
  297.6 1.2 bitcast_add_fusion.2
  298.9 1.1 copy-done.3
  300.0 2.3 collective-permute-start.3
  302.4 35.1 %collective-permute-done.3 = bf16[1,80,2048]{2,1,0:T(8,128)(2,1)S(1)} collective-permute-done((bf16[1,80,2048]{2,1,0:T(8,128)(2,1)S(1)}, bf16[1,80,2048]{2,1,0:T(8,128)(2,1)S(1)}, u32[]{:S(2)}, u32[]{:S(2)}) %collective-permute-start.3) | collective-permute-done | bytes 327712 | tf_op jit(solution)/shard_map/ppermute | solution.py:20
  337.5 1.1 convert_add_fusion.1
  338.7 3.7 all-to-all-start.3
  344.1 1.9 collective-permute-start.5
  346.0 5.7 %collective-permute-done.5 = bf16[2,4,2048]{2,1,0:T(4,128)(2,1)S(1)} collective-permute-done((bf16[2,4,2048]{2,1,0:T(4,128)(2,1)S(1)}, bf16[2,4,2048]{2,1,0:T(4,128)(2,1)S(1)}, u32[]{:S(2)}, u32[]{:S(2)}) %collective-permute-start.5) | collective-permute-done | bytes 32800 | tf_op jit(solution)/shard_map/ppermute | solution.py:20
  351.8 9.5 %collective-permute-done.6 = bf16[2,4,2048]{2,1,0:T(4,128)(2,1)S(1)} collective-permute-done((bf16[2,4,2048]{2,1,0:T(4,128)(2,1)S(1)}, bf16[2,4,2048]{2,1,0:T(4,128)(2,1)S(1)}, u32[]{:S(2)}, u32[]{:S(2)}) %collective-permute-start.6) | collective-permute-done | bytes 32800 | tf_op jit(solution)/shard_map/ppermute | solution.py:20
  361.3 4.5 %collective-permute-start.7 = (bf16[2,4,2048]{2,1,0:T(4,128)(2,1)S(1)}, bf16[2,4,2048]{2,1,0:T(4,128)(2,1)S(1)}, u32[]{:S(2)}, u32[]{:S(2)}) collective-permute-start(bf16[2,4,2048]{2,1,0:T(4,128)(2,1)S(1)} %add.202), channel_id=1, source_target_pairs={{0,8},{1,9},{2,10},{3,11},{4,12},{5,13},{6,14},{7,15},{8,0},{9,1},... | collective-permute-start | bytes 98312 | tf_op jit(solution)/shard_map/ppermute | solution.py:20
  365.8 1.8 gather_fusion.1
  367.6 2.8 collective-permute-done.7
  371.2 1.1 broadcast_select_fusion.2
  372.3 2.6 collective-permute-done.8
  375.4 3.7 all-to-all-start.5
  379.1 3.9 fusion.47
  384.5 1.9 collective-permute-start.10
  386.4 1.7 collective-permute-done.10
  388.2 1.9 collective-permute-start.11
  390.1 7.2 %collective-permute-done.11 = f32[2,16]{1,0:T(2,128)S(1)} collective-permute-done((f32[2,16]{1,0:T(2,128)S(1)}, f32[2,16]{1,0:T(2,128)S(1)}, u32[]{:S(2)}, u32[]{:S(2)}) %collective-permute-start.11) | collective-permute-done | bytes 160 | tf_op jit(solution)/shard_map/ppermute | solution.py:20
  397.3 4.4 %collective-permute-start.12 = (f32[2,16]{1,0:T(2,128)S(1)}, f32[2,16]{1,0:T(2,128)S(1)}, u32[]{:S(2)}, u32[]{:S(2)}) collective-permute-start(f32[2,16]{1,0:T(2,128)S(1)} %pad_maximum_fusion.4), channel_id=1, source_target_pairs={{0,8},{1,9},{2,10},{3,11},{4,12},{5,13},{6,14},{7,15},{8,0},{9,1},... | collective-permute-start | bytes 392 | tf_op jit(solution)/shard_map/ppermute | solution.py:20
  401.7 4.0 collective-permute-done.12
  406.4 3.0 collective-permute-done.13
  410.1 2.3 copy.33
  (89 shorter events, 14.6 us)
Async XLA Ops:
  7.2 64.8 %all-gather.8.cloned.1.call-start = ((), (), s32[]{:S(2)}) async-start(), calls=%async_computation.6 | async-start | bytes 5918720 | tf_op jit(solution)/shard_map/all_gather | solution.py:97
  11.3 93.9 %all-gather.10.cloned.1.call-start = ((), (), s32[]{:S(2)}) async-start(), calls=%async_computation.7 | async-start | bytes 3145728 | tf_op jit(solution)/shard_map/all_gather | solution.py:98
  12.1 127.8 %all-gather.14.cloned.1.call-start = ((), (), s32[]{:S(2)}) async-start(), calls=%async_computation.9 | async-start | bytes 3145728 | tf_op jit(solution)/shard_map/all_gather | solution.py:100
  12.8 161.7 %all-gather.12.cloned.1.call-start = ((), (), s32[]{:S(2)}) async-start(), calls=%async_computation.8 | async-start | bytes 3145728 | tf_op jit(solution)/shard_map/all_gather | solution.py:99
  185.9 4.5 %copy-start.2 = (bf16[1,1024,512]{2,1,0:T(8,128)(2,1)S(1)}, bf16[1,1024,512]{2,1,0:T(8,128)(2,1)}, u32[]{:S(2)}) copy-start(bf16[1,1024,512]{2,1,0:T(8,128)(2,1)} %param.20) | copy-start | bytes 3145732
  190.3 35.5 %collective-permute-start = (bf16[8,80,2048]{2,1,0:T(8,128)(2,1)}, bf16[8,80,2048]{2,1,0:T(8,128)(2,1)}, u32[]{:S(2)}, u32[]{:S(2)}) collective-permute-start(bf16[8,80,2048]{2,1,0:T(8,128)(2,1)} %fusion.10), channel_id=1, source_target_pairs={{0,1},{1,0},{2,3},{3,2},{4,5},{5,4},{6,7},{7,6},{8,9},{9,8},{10,11... | collective-permute-start | bytes 7864328 | tf_op jit(solution)/shard_map/ppermute | solution.py:20
  220.8 28.0 %all-to-all-start = ((bf16[16,64,512]{2,1,0:T(8,128)(2,1)}), bf16[16,64,512]{2,1,0:T(8,128)(2,1)S(1)}, u32[]{:S(2)}, u32[]{:S(2)}) async-start(bf16[16,64,512]{2,1,0:T(8,128)(2,1)} %bitcast.14), calls=%async_computation | async-start | bytes 2097152 | tf_op jit(solution)/shard_map/all_to_all | solution.py:26
  230.0 2.3 copy-start
  230.0 25.9 %copy-start.9 = (s32[16]{0:T(128)S(1)}, s32[16]{0:T(128)}, u32[]{:S(2)}) copy-start(s32[16]{0:T(128)} %param.23) | copy-start | bytes 196
  230.0 25.9 %copy-start.8 = (s32[16]{0:T(128)S(1)}, s32[16]{0:T(128)}, u32[]{:S(2)}) copy-start(s32[16]{0:T(128)} %param.22) | copy-start | bytes 196
  232.5 43.6 %collective-permute-start.1 = (bf16[4,80,2048]{2,1,0:T(8,128)(2,1)S(1)}, bf16[4,80,2048]{2,1,0:T(8,128)(2,1)}, u32[]{:S(2)}, u32[]{:S(2)}) collective-permute-start(bf16[4,80,2048]{2,1,0:T(8,128)(2,1)S(1)} %fusion.14), channel_id=1, source_target_pairs={{0,2},{1,3},{2,0},{3,1},{4,6},{5,7},{6,4},{7,5},{8,10},{9,11},{10,... | collective-permute-start | bytes 3932168 | tf_op jit(solution)/shard_map/ppermute | solution.py:20
  248.8 7.1 %copy-start.1 = (bf16[16,64,512]{2,1,0:T(8,128)(2,1)}, bf16[16,64,512]{2,1,0:T(8,128)(2,1)S(1)}, u32[]{:S(2)}) copy-start(bf16[16,64,512]{2,1,0:T(8,128)(2,1)S(1)} %all-to-all-done) | copy-start | bytes 3145732
  248.8 43.1 %all-to-all-start.4 = ((bf16[16,16,2048]{2,1,0:T(8,128)(2,1)}), bf16[16,16,2048]{2,1,0:T(8,128)(2,1)}, u32[]{:S(2)}, u32[]{:S(2)}) async-start(bf16[16,16,2048]{2,1,0:T(8,128)(2,1)} %bitcast.18), calls=%async_computation.4 | async-start | bytes 2097152 | tf_op jit(solution)/shard_map/all_to_all | solution.py:26
  279.5 18.2 %collective-permute-start.2 = (bf16[2,80,2048]{2,1,0:T(8,128)(2,1)}, bf16[2,80,2048]{2,1,0:T(8,128)(2,1)}, u32[]{:S(2)}, u32[]{:S(2)}) collective-permute-start(bf16[2,80,2048]{2,1,0:T(8,128)(2,1)} %fusion.24), channel_id=1, source_target_pairs={{0,4},{1,5},{2,6},{3,7},{4,0},{5,1},{6,2},{7,3},{8,12},{9,13},{10,... | collective-permute-start | bytes 1966088 | tf_op jit(solution)/shard_map/ppermute | solution.py:20
  291.9 10.3 %copy-start.7 = (s32[2,1,4]{2,1,0:T(1,128)S(1)}, s32[2,1,4]{2,1,0:T(1,128)}, u32[]{:S(2)}) copy-start(s32[2,1,4]{2,1,0:T(1,128)} %param.24) | copy-start | bytes 100
  291.9 46.9 %all-to-all-start.1 = ((bf16[16,64,512]{2,1,0:T(8,128)(2,1)}), bf16[16,64,512]{2,1,0:T(8,128)(2,1)}, u32[]{:S(2)}, u32[]{:S(2)}) async-start(bf16[16,64,512]{2,1,0:T(8,128)(2,1)} %get-tuple-element.22), calls=%async_computation.1 | async-start | bytes 2097152 | tf_op jit(solution)/shard_map/all_to_all | solution.py:28
  297.0 41.7 %copy-start.4 = (bf16[2,40,2048]{2,1,0:T(8,128)(2,1)S(1)}, bf16[2,40,2048]{2,1,0:T(8,128)(2,1)}, u32[]{:S(2)}) copy-start(bf16[2,40,2048]{2,1,0:T(8,128)(2,1)} %param.14) | copy-start | bytes 983044
  298.8 1.1 copy-start.3
  300.0 37.5 %collective-permute-start.3 = (bf16[1,80,2048]{2,1,0:T(8,128)(2,1)S(1)}, bf16[1,80,2048]{2,1,0:T(8,128)(2,1)S(1)}, u32[]{:S(2)}, u32[]{:S(2)}) collective-permute-start(bf16[1,80,2048]{2,1,0:T(8,128)(2,1)S(1)} %dynamic-slice_convert_fusion.2), channel_id=1, source_target_pairs={{0,8},{1,9},{2,10},{3,11},{4,12},{5,13},{6,14},{7,15},{8,0},{9,1},... | collective-permute-start | bytes 983048 | tf_op jit(solution)/shard_map/ppermute | solution.py:20
  338.7 33.6 %copy-start.5 = (bf16[2,40,2048]{2,1,0:T(8,128)(2,1)}, bf16[2,40,2048]{2,1,0:T(8,128)(2,1)S(1)}, u32[]{:S(2)}) copy-start(bf16[2,40,2048]{2,1,0:T(8,128)(2,1)S(1)} %fusion.23) | copy-start | bytes 983044
  338.7 36.6 %all-to-all-start.3 = ((bf16[16,64,512]{2,1,0:T(8,128)(2,1)}), bf16[16,64,512]{2,1,0:T(8,128)(2,1)S(1)}, u32[]{:S(2)}, u32[]{:S(2)}) async-start(bf16[16,64,512]{2,1,0:T(8,128)(2,1)} %get-tuple-element.21), calls=%async_computation.3 | async-start | bytes 2097152 | tf_op jit(solution)/shard_map/all_to_all | solution.py:28
  342.7 1.3 collective-permute-start.4
  344.1 7.6 %collective-permute-start.5 = (bf16[2,4,2048]{2,1,0:T(4,128)(2,1)S(1)}, bf16[2,4,2048]{2,1,0:T(4,128)(2,1)S(1)}, u32[]{:S(2)}, u32[]{:S(2)}) collective-permute-start(bf16[2,4,2048]{2,1,0:T(4,128)(2,1)S(1)} %add.200), channel_id=1, source_target_pairs={{0,2},{1,3},{2,0},{3,1},{4,6},{5,7},{6,4},{7,5},{8,10},{9,11},{10,... | collective-permute-start | bytes 98312 | tf_op jit(solution)/shard_map/ppermute | solution.py:20
  351.8 9.5 %collective-permute-start.6 = (bf16[2,4,2048]{2,1,0:T(4,128)(2,1)S(1)}, bf16[2,4,2048]{2,1,0:T(4,128)(2,1)S(1)}, u32[]{:S(2)}, u32[]{:S(2)}) collective-permute-start(bf16[2,4,2048]{2,1,0:T(4,128)(2,1)S(1)} %add.201), channel_id=1, source_target_pairs={{0,4},{1,5},{2,6},{3,7},{4,0},{5,1},{6,2},{7,3},{8,12},{9,13},{10,... | collective-permute-start | bytes 98312 | tf_op jit(solution)/shard_map/ppermute | solution.py:20
  361.3 9.1 %collective-permute-start.7 = (bf16[2,4,2048]{2,1,0:T(4,128)(2,1)S(1)}, bf16[2,4,2048]{2,1,0:T(4,128)(2,1)S(1)}, u32[]{:S(2)}, u32[]{:S(2)}) collective-permute-start(bf16[2,4,2048]{2,1,0:T(4,128)(2,1)S(1)} %add.202), channel_id=1, source_target_pairs={{0,8},{1,9},{2,10},{3,11},{4,12},{5,13},{6,14},{7,15},{8,0},{9,1},... | collective-permute-start | bytes 98312 | tf_op jit(solution)/shard_map/ppermute | solution.py:20
  367.6 11.5 %copy-start.6 = (f32[2048]{0:T(1024)S(1)}, f32[2048]{0:T(1024)}, u32[]{:S(2)}) copy-start(f32[2048]{0:T(1024)} %param.18) | copy-start | bytes 24580
  370.6 4.3 %collective-permute-start.8 = (bf16[2,2,4,2048]{3,2,1,0:T(4,128)(2,1)S(1)}, bf16[2,2,4,2048]{3,2,1,0:T(4,128)(2,1)S(1)}, u32[]{:S(2)}, u32[]{:S(2)}) collective-permute-start(bf16[2,2,4,2048]{3,2,1,0:T(4,128)(2,1)S(1)} %broadcast_select_fusion.3), channel_id=1, source_target_pairs={{0,16},{16,0},{1,17},{17,1},{2,18},{18,2},{3,19},{19,3},{4,20},{20... | collective-permute-start | bytes 196616 | tf_op jit(solution)/shard_map/ppermute | solution.py:20
  375.4 31.0 %all-to-all-start.5 = ((bf16[16,16,2048]{2,1,0:T(8,128)(2,1)}), bf16[16,16,2048]{2,1,0:T(8,128)(2,1)S(1)}, u32[]{:S(2)}, u32[]{:S(2)}) async-start(bf16[16,16,2048]{2,1,0:T(8,128)(2,1)} %broadcast_select_fusion.2), calls=%async_computation.5 | async-start | bytes 2097152 | tf_op jit(solution)/shard_map/all_to_all | solution.py:28
  383.2 1.3 collective-permute-start.9
  384.5 3.6 collective-permute-start.10
  388.2 9.1 %collective-permute-start.11 = (f32[2,16]{1,0:T(2,128)S(1)}, f32[2,16]{1,0:T(2,128)S(1)}, u32[]{:S(2)}, u32[]{:S(2)}) collective-permute-start(f32[2,16]{1,0:T(2,128)S(1)} %pad_maximum_fusion.3), channel_id=1, source_target_pairs={{0,4},{1,5},{2,6},{3,7},{4,0},{5,1},{6,2},{7,3},{8,12},{9,13},{10,... | collective-permute-start | bytes 392 | tf_op jit(solution)/shard_map/ppermute | solution.py:20
  397.3 8.4 %collective-permute-start.12 = (f32[2,16]{1,0:T(2,128)S(1)}, f32[2,16]{1,0:T(2,128)S(1)}, u32[]{:S(2)}, u32[]{:S(2)}) collective-permute-start(f32[2,16]{1,0:T(2,128)S(1)} %pad_maximum_fusion.4), channel_id=1, source_target_pairs={{0,8},{1,9},{2,10},{3,11},{4,12},{5,13},{6,14},{7,15},{8,0},{9,1},... | collective-permute-start | bytes 392 | tf_op jit(solution)/shard_map/ppermute | solution.py:20
  405.7 3.6 collective-permute-start.13
Sparse Core Ops, SparseCore 0:
  11.4 60.4 all-gather.7
  73.5 31.6 all-gather.9
  106.7 33.1 all-gather.13
  141.3 33.1 all-gather.11
where the time goes:
time: 422 us; the launch traced here: 421 us
  waiting for transfers between devices  264 us (63%)
  starting transfers between devices  49.4 us (12%)
  blocking collectives  30.5 us (7%)
  local copies, waits for them, and re-layouts  21.7 us (5%)
  matrix products  20.9 us (5%)
  other arithmetic  20.1 us (5%)
  between operations  14.3 us (3%)
    ppermute x14, waiting for transfers between devices, exchange(): return lax.ppermute(value, axis, [(i, i ^ bit) for i in range(n)])  93.3 us
    all_gather x1, waiting for transfers between devices, per_device(): lax.all_gather(jnp.concatenate([normed, coded], axis=1), 'ep', axis=0, ti...  58.4 us
    all_gather x1, waiting for transfers between devices, per_device(): up_full = lax.all_gather(up_proj[0], 'grp', axis=0, tiled=True)  34.6 us
    all_gather x1, waiting for transfers between devices, per_device(): gate_full = lax.all_gather(gate_proj[0], 'grp', axis=0, tiled=True)  32.1 us
    all_to_all x1, blocking collectives, relocate(): spread = lax.all_to_all(rows, 'ep', split_axis=0, concat_axis=0, tiled=True)  30.5 us
    all_gather x1, waiting for transfers between devices, per_device(): down_full = lax.all_gather(down_proj[0], 'grp', axis=0, tiled=True)  29.3 us
    ppermute x14, starting transfers between devices, exchange(): return lax.ppermute(value, axis, [(i, i ^ bit) for i in range(n)])  24.7 us
    all_to_all x2, waiting for transfers between devices, relocate(): spread = lax.all_to_all(rows, 'ep', split_axis=0, concat_axis=0, tiled=True)  14.4 us
  transfers between devices with their start and end apart: 23, of which 18 were waited for; matrix products, arithmetic and copies ran while one was open for 8% of the time, Pallas kernels for 0%

commit v1 on v0

--- a/solution.py
+++ b/solution.py
@@ -94,7 +94,31 @@
     parts = split_bf16(slot_gates.reshape(-1, n_slots))
     extra = -(-len(parts) * n_slots // 128) * 128
     coded = jnp.pad(jnp.concatenate(parts, axis=1), ((0, 0), (0, extra - len(parts) * n_slots)))
-    rows = lax.all_gather(jnp.concatenate([normed, coded], axis=1), "ep", axis=0, tiled=True)
+
+    def change_packet(load):
+        reply, outer, x_now = (lax.axis_size("ep"), lax.axis_index("ep"), load.shape[0])
+        row_list = [pp * reply if no == 0 else pp for no, pp in enumerate(load.shape)]
+        near = lax.dynamic_update_slice_in_dim(
+            jnp.zeros(row_list, load.dtype), load, outer * x_now, axis=0
+        )
+        current_block = back = load
+        for k0 in range(1, reply // 2 + 1):
+            current_block = lax.ppermute(
+                current_block, axis_name="ep", perm=[(no, (no + 1) % reply) for no in range(reply)]
+            )
+            near = lax.dynamic_update_slice_in_dim(
+                near, current_block, (outer - k0) % reply * x_now, axis=0
+            )
+            if 2 * k0 < reply:
+                back = lax.ppermute(
+                    back, axis_name="ep", perm=[(no, (no - 1) % reply) for no in range(reply)]
+                )
+                near = lax.dynamic_update_slice_in_dim(
+                    near, back, (outer + k0) % reply * x_now, axis=0
+                )
+        return near
+
+    rows = change_packet(jnp.concatenate([normed, coded], axis=1))
     gate_full = lax.all_gather(gate_proj[0], "grp", axis=0, tiled=True)
     up_full = lax.all_gather(up_proj[0], "grp", axis=0, tiled=True)
     down_full = lax.all_gather(down_proj[0], "grp", axis=0, tiled=True)

time: 422 us -> 362 us (0.86)
  waiting for transfers between devices: 264 us -> 154 us
  starting transfers between devices: 49.4 us -> 85 us
  local copies, waits for them, and re-layouts: 21.7 us -> 36 us
    all_gather x1 -> x0, waiting for transfers between devices: 58.4 us -> none  [per_device(): lax.all_gather(jnp.concatenate([normed, coded], axis=1), 'ep', axis=0, ti...]
    ppermute x0 -> x15, starting transfers between devices: none -> 35.9 us  [the longest x7 21.6 us: change_packet(): lax.ppermute(back, axis_name='ep', perm=[(no, (no - 1) % reply) for no in...]
    all_gather x1, waiting for transfers between devices: 32.1 us -> 0.02 us  [per_device(): gate_full = lax.all_gather(gate_proj[0], 'grp', axis=0, tiled=True)]
    ppermute x0 -> x15, waiting for transfers between devices: none -> 30.1 us  [the longest x8 30 us: change_packet(): lax.ppermute(current_block, axis_name='ep', perm=[(no, (no + 1) % reply)...]
    all_gather x1, waiting for transfers between devices: 29.3 us -> 0.02 us  [per_device(): down_full = lax.all_gather(down_proj[0], 'grp', axis=0, tiled=True)]
    all_gather x1, waiting for transfers between devices: 34.6 us -> 14.7 us  [per_device(): up_full = lax.all_gather(up_proj[0], 'grp', axis=0, tiled=True)]
    dynamic_update_slice x0 -> x15, local copies, waits for them, and re-layouts: none -> 11.5 us  [the longest x8 6.11 us: change_packet(): lax.dynamic_update_slice_in_dim(near, current_block, (outer - k0) % reply...]
  transfers between devices with their start and end apart: 23 -> 37, of which waited for: 18 -> 23; matrix products, arithmetic and copies ran while one was open for 8% -> 15% of each run, Pallas kernels for 0% -> 0%
where the time goes in v1:
time: 362 us; the launch traced here: 361 us
  waiting for transfers between devices  154 us (43%)
  starting transfers between devices  85 us (23%)
  local copies, waits for them, and re-layouts  36 us (10%)
  blocking collectives  30.5 us (8%)
  matrix products  20.9 us (6%)
  other arithmetic  20.2 us (6%)
  between operations  14.6 us (4%)
    ppermute x14, waiting for transfers between devices, exchange(): return lax.ppermute(value, axis, [(i, i ^ bit) for i in range(n)])  93.4 us
    all_to_all x1, blocking collectives, relocate(): spread = lax.all_to_all(rows, 'ep', split_axis=0, concat_axis=0, tiled=True)  30.5 us
    ppermute x8, waiting for transfers between devices, change_packet(): lax.ppermute(current_block, axis_name='ep', perm=[(no, (no + 1) % reply)...  30 us
    ppermute x14, starting transfers between devices, exchange(): return lax.ppermute(value, axis, [(i, i ^ bit) for i in range(n)])  24.5 us
    ppermute x7, starting transfers between devices, change_packet(): lax.ppermute(back, axis_name='ep', perm=[(no, (no - 1) % reply) for no in...  21.6 us
    all_gather x1, waiting for transfers between devices, per_device(): up_full = lax.all_gather(up_proj[0], 'grp', axis=0, tiled=True)  14.7 us
    all_to_all x2, waiting for transfers between devices, relocate(): spread = lax.all_to_all(rows, 'ep', split_axis=0, concat_axis=0, tiled=True)  14.4 us
    ppermute x8, starting transfers between devices, change_packet(): lax.ppermute(current_block, axis_name='ep', perm=[(no, (no + 1) % reply)...  14.2 us
  transfers between devices with their start and end apart: 37, of which 23 were waited for; matrix products, arithmetic and copies ran while one was open for 15% of the time, Pallas kernels for 0%

profile of v1, /device:TPU:0, one launch (start us, length us, event | category | flops | bytes accessed | tf_op | source)
XLA Modules:
  0.0 361.2 jit_solution(5984902093367620109)
XLA Ops:
  12.0 2.8 broadcast_in_dim.99
  16.0 5.0 %collective-permute-start.1 = (bf16[80,2176]{1,0:T(8,128)(2,1)S(1)}, bf16[80,2176]{1,0:T(8,128)(2,1)S(1)}, u32[]{:S(2)}, u32[]{:S(2)}) collective-permute-start(bf16[80,2176]{1,0:T(8,128)(2,1)S(1)} %get-tuple-element.16), channel_id=1, source_target_pairs={{0,15},{1,0},{2,1},{3,2},{4,3},{5,4},{6,5},{7,6},{8,7},{9,8},{10,9... | collective-permute-start | bytes 1044488 | tf_op jit(solution)/shard_map/ppermute | solution.py:113
  21.4 4.7 %collective-permute-done = bf16[80,2176]{1,0:T(8,128)(2,1)S(1)} collective-permute-done((bf16[80,2176]{1,0:T(8,128)(2,1)S(1)}, bf16[80,2176]{1,0:T(8,128)(2,1)S(1)}, u32[]{:S(2)}, u32[]{:S(2)}) %collective-permute-start) | collective-permute-done | bytes 348192 | tf_op jit(solution)/shard_map/ppermute | solution.py:106
  26.6 3.9 %collective-permute-start.3 = (bf16[80,2176]{1,0:T(8,128)(2,1)S(1)}, bf16[80,2176]{1,0:T(8,128)(2,1)S(1)}, u32[]{:S(2)}, u32[]{:S(2)}) collective-permute-start(bf16[80,2176]{1,0:T(8,128)(2,1)S(1)} %collective-permute-done.1), channel_id=1, source_target_pairs={{0,15},{1,0},{2,1},{3,2},{4,3},{5,4},{6,5},{7,6},{8,7},{9,8},{10,9... | collective-permute-start | bytes 1044488 | tf_op jit(solution)/shard_map/ppermute | solution.py:113
  32.1 3.5 collective-permute-done.2
  37.0 3.0 collective-permute-start.5
  41.6 3.6 collective-permute-done.4
  46.7 2.9 collective-permute-start.7
  51.1 3.5 collective-permute-done.6
  56.4 2.7 collective-permute-start.9
  60.7 3.5 collective-permute-done.8
  66.1 2.5 collective-permute-start.11
  70.1 3.5 collective-permute-done.10
  73.7 2.8 collective-permute-start.12
  79.7 3.5 collective-permute-done.12
  83.2 3.7 %collective-permute-start.14 = (bf16[80,2176]{1,0:T(8,128)(2,1)S(1)}, bf16[80,2176]{1,0:T(8,128)(2,1)S(1)}, u32[]{:S(2)}, u32[]{:S(2)}) collective-permute-start(bf16[80,2176]{1,0:T(8,128)(2,1)S(1)} %collective-permute-done.12), channel_id=1, source_target_pairs={{0,1},{1,2},{2,3},{3,4},{4,5},{5,6},{6,7},{7,8},{8,9},{9,10},{10,1... | collective-permute-start | bytes 1044488 | tf_op jit(solution)/shard_map/ppermute | solution.py:106
  88.4 4.2 %collective-permute-done.14 = bf16[80,2176]{1,0:T(8,128)(2,1)S(1)} collective-permute-done((bf16[80,2176]{1,0:T(8,128)(2,1)S(1)}, bf16[80,2176]{1,0:T(8,128)(2,1)S(1)}, u32[]{:S(2)}, u32[]{:S(2)}) %collective-permute-start.14) | collective-permute-done | bytes 348192 | tf_op jit(solution)/shard_map/ppermute | solution.py:106
  94.6 5.4 %fusion.2 = f32[1280,512]{1,0:T(8,128)S(1)} fusion(bf16[1280,2176]{1,0:T(8,128)(2,1)} %constant_dynamic-update-slice_fusion, bf16[1,2048,512]{2,1,0:T(8,128)(2,1)} %all-gather.7.cloned.1.call-done), kind=kOutput, calls=%fused_computation.9 | convolution fusion | flops 2684354560 | bytes 9961472 | tf_op jit(solution)/shard_map/dot_general | solution.py:130
  100.0 14.7 %all-gather.9.cloned.1.call-done = bf16[1,2048,512]{2,1,0:T(8,128)(2,1)} async-done(((bf16[1,1024,512]{2,1,0:T(8,128)(2,1)}), bf16[1,2048,512]{2,1,0:T(8,128)(2,1)}) %all-gather.9.cloned.1.call-update) | async-done | bytes 2097168 | tf_op jit(solution)/shard_map/all_gather | solution.py:123
  114.8 11.4 %convolution_multiply_fusion = f32[1280,2048]{1,0:T(8,128)} fusion(f32[1280]{0:T(1024)S(1)} %select_reduce_fusion, bf16[1,512,2048]{2,1,0:T(8,128)(2,1)} %all-gather.11.cloned.1.call-done, f32[1280,512]{1,0:T(8,128)S(1)} %fusion.2, bf16[1,2048,512]{2,1,0:T(8,128)(2,1)} %all-gather.9.cloned.1.call-done, bf16[1280,2176]{1,0:T(8,128)(2,1)} %constant_dynamic-update-slice_fusion), kind=kOutput, calls=%fused_computation.4 | convolution fusion | flops 5375262720 | bytes 22549504 | tf_op jit(solution)/shard_map/dot_general | solution.py:133
  126.2 4.5 %fusion.4 = bf16[8,80,2048]{2,1,0:T(8,128)(2,1)} fusion(f32[8,2,80,2048]{3,2,1,0:T(8,128)} %bitcast.151, s32[]{:T(128)S(6)} %select_n.251), kind=kLoop, calls=%fused_computation.11 | loop fusion | bytes 5242884 | tf_op jit(solution)/shard_map/convert_element_type | solution.py:49
  130.7 30.5 %all_to_all.30 = bf16[16,64,512]{2,1,0:T(8,128)(2,1)} all-to-all(bf16[16,64,512]{2,1,0:T(8,128)(2,1)S(1)} %bitcast.153), channel_id=1, replica_groups=mesh['grp'=2,'ep'=16] {'ep'}, dimensions={0} | all-to-all | bytes 2097152 | tf_op jit(solution)/shard_map/all_to_all | solution.py:26
  161.2 5.0 %all-to-all-start.2 = ((bf16[16,64,512]{2,1,0:T(8,128)(2,1)}), bf16[16,64,512]{2,1,0:T(8,128)(2,1)S(1)}, u32[]{:S(2)}, u32[]{:S(2)}) async-start(bf16[16,64,512]{2,1,0:T(8,128)(2,1)} %bitcast.16), calls=%async_computation.2 | async-start | bytes 2097152 | tf_op jit(solution)/shard_map/all_to_all | solution.py:26
  166.2 4.1 %bitcast_add_fusion = f32[8,80,2048]{2,1,0:T(8,128)S(1)} fusion(bf16[8,80,2048]{2,1,0:T(8,128)(2,1)} %collective-permute-done.15, f32[8,2,80,2048]{3,2,1,0:T(8,128)} %bitcast.152, s32[]{:T(128)S(6)} %select_n.250), kind=kLoop, calls=%fused_computation.6 | loop fusion | flops 2621440 | bytes 13107204 | tf_op jit(solution)/shard_map/add | solution.py:49
  170.4 2.3 copy-done
  174.8 14.3 %all-to-all-done.2 = bf16[16,64,512]{2,1,0:T(8,128)(2,1)S(1)} async-done(((bf16[16,64,512]{2,1,0:T(8,128)(2,1)}), bf16[16,64,512]{2,1,0:T(8,128)(2,1)S(1)}, u32[]{:S(2)}, u32[]{:S(2)}) %all-to-all-start.2) | async-done | bytes 1048608 | tf_op jit(solution)/shard_map/all_to_all | solution.py:26
  189.2 7.0 %all-to-all-start.4 = ((bf16[16,16,2048]{2,1,0:T(8,128)(2,1)}), bf16[16,16,2048]{2,1,0:T(8,128)(2,1)}, u32[]{:S(2)}, u32[]{:S(2)}) async-start(bf16[16,16,2048]{2,1,0:T(8,128)(2,1)} %bitcast.18), calls=%async_computation.4 | async-start | bytes 2097152 | tf_op jit(solution)/shard_map/all_to_all | solution.py:26
  197.0 19.4 %collective-permute-done.16 = bf16[4,80,2048]{2,1,0:T(8,128)(2,1)} collective-permute-done((bf16[4,80,2048]{2,1,0:T(8,128)(2,1)S(1)}, bf16[4,80,2048]{2,1,0:T(8,128)(2,1)}, u32[]{:S(2)}, u32[]{:S(2)}) %collective-permute-start.16) | collective-permute-done | bytes 1310752 | tf_op jit(solution)/shard_map/ppermute | solution.py:20
  216.4 2.4 bitcast_add_fusion.1
  219.8 3.7 %collective-permute-start.17 = (bf16[2,80,2048]{2,1,0:T(8,128)(2,1)}, bf16[2,80,2048]{2,1,0:T(8,128)(2,1)}, u32[]{:S(2)}, u32[]{:S(2)}) collective-permute-start(bf16[2,80,2048]{2,1,0:T(8,128)(2,1)} %fusion.22), channel_id=1, source_target_pairs={{0,4},{1,5},{2,6},{3,7},{4,0},{5,1},{6,2},{7,3},{8,12},{9,13},{10,... | collective-permute-start | bytes 1966088 | tf_op jit(solution)/shard_map/ppermute | solution.py:20
  223.5 2.8 gather_fusion.2
  226.3 2.8 gather_fusion.3
  229.1 3.2 broadcast_select_fusion
  232.3 4.9 %all-to-all-start.1 = ((bf16[16,64,512]{2,1,0:T(8,128)(2,1)}), bf16[16,64,512]{2,1,0:T(8,128)(2,1)}, u32[]{:S(2)}, u32[]{:S(2)}) async-start(bf16[16,64,512]{2,1,0:T(8,128)(2,1)} %get-tuple-element.24), calls=%async_computation.1 | async-start | bytes 2097152 | tf_op jit(solution)/shard_map/all_to_all | solution.py:28
  242.6 35.1 %collective-permute-done.18 = bf16[1,80,2048]{2,1,0:T(8,128)(2,1)S(1)} collective-permute-done((bf16[1,80,2048]{2,1,0:T(8,128)(2,1)S(1)}, bf16[1,80,2048]{2,1,0:T(8,128)(2,1)S(1)}, u32[]{:S(2)}, u32[]{:S(2)}) %collective-permute-start.18) | collective-permute-done | bytes 327712 | tf_op jit(solution)/shard_map/ppermute | solution.py:20
  279.0 3.9 %all-to-all-start.3 = ((bf16[16,64,512]{2,1,0:T(8,128)(2,1)}), bf16[16,64,512]{2,1,0:T(8,128)(2,1)S(1)}, u32[]{:S(2)}, u32[]{:S(2)}) async-start(bf16[16,64,512]{2,1,0:T(8,128)(2,1)} %get-tuple-element.23), calls=%async_computation.3 | async-start | bytes 2097152 | tf_op jit(solution)/shard_map/all_to_all | solution.py:28
  286.3 5.7 %collective-permute-done.20 = bf16[2,4,2048]{2,1,0:T(4,128)(2,1)S(1)} collective-permute-done((bf16[2,4,2048]{2,1,0:T(4,128)(2,1)S(1)}, bf16[2,4,2048]{2,1,0:T(4,128)(2,1)S(1)}, u32[]{:S(2)}, u32[]{:S(2)}) %collective-permute-start.20) | collective-permute-done | bytes 32800 | tf_op jit(solution)/shard_map/ppermute | solution.py:20
  292.1 9.4 %collective-permute-done.21 = bf16[2,4,2048]{2,1,0:T(4,128)(2,1)S(1)} collective-permute-done((bf16[2,4,2048]{2,1,0:T(4,128)(2,1)S(1)}, bf16[2,4,2048]{2,1,0:T(4,128)(2,1)S(1)}, u32[]{:S(2)}, u32[]{:S(2)}) %collective-permute-start.21) | collective-permute-done | bytes 32800 | tf_op jit(solution)/shard_map/ppermute | solution.py:20
  301.5 4.6 %collective-permute-start.22 = (bf16[2,4,2048]{2,1,0:T(4,128)(2,1)S(1)}, bf16[2,4,2048]{2,1,0:T(4,128)(2,1)S(1)}, u32[]{:S(2)}, u32[]{:S(2)}) collective-permute-start(bf16[2,4,2048]{2,1,0:T(4,128)(2,1)S(1)} %add.362), channel_id=1, source_target_pairs={{0,8},{1,9},{2,10},{3,11},{4,12},{5,13},{6,14},{7,15},{8,0},{9,1},... | collective-permute-start | bytes 98312 | tf_op jit(solution)/shard_map/ppermute | solution.py:20
  307.9 2.8 collective-permute-done.22
  312.6 2.6 collective-permute-done.23
  315.7 3.7 %all-to-all-start.5 = ((bf16[16,16,2048]{2,1,0:T(8,128)(2,1)}), bf16[16,16,2048]{2,1,0:T(8,128)(2,1)S(1)}, u32[]{:S(2)}, u32[]{:S(2)}) async-start(bf16[16,16,2048]{2,1,0:T(8,128)(2,1)} %broadcast_select_fusion.2), calls=%async_computation.5 | async-start | bytes 2097152 | tf_op jit(solution)/shard_map/all_to_all | solution.py:28
  319.4 3.9 %fusion.45 = (f32[16]{0:T(128)S(1)}, f32[16,1536]{1,0:T(8,128)S(1)}) fusion(bf16[2048,1536]{1,0:T(8,128)(2,1)} %param.25, f32[16,2048]{1,0:T(8,128)S(1)} %reshape.265, f32[2048]{0:T(1024)S(1)} %copy-done.6, f32[16]{0:T(128)S(1)} %rsqrt.21), kind=kOutput, calls=%fused_computation.130 | convolution fusion | flops 100786160 | bytes 6529152 | tf_op jit(solution)/shard_map/dot_general | solution.py:152
  330.4 7.2 %collective-permute-done.26 = f32[2,16]{1,0:T(2,128)S(1)} collective-permute-done((f32[2,16]{1,0:T(2,128)S(1)}, f32[2,16]{1,0:T(2,128)S(1)}, u32[]{:S(2)}, u32[]{:S(2)}) %collective-permute-start.26) | collective-permute-done | bytes 160 | tf_op jit(solution)/shard_map/ppermute | solution.py:20
  337.6 4.4 %collective-permute-start.27 = (f32[2,16]{1,0:T(2,128)S(1)}, f32[2,16]{1,0:T(2,128)S(1)}, u32[]{:S(2)}, u32[]{:S(2)}) collective-permute-start(f32[2,16]{1,0:T(2,128)S(1)} %pad_maximum_fusion.4), channel_id=1, source_target_pairs={{0,8},{1,9},{2,10},{3,11},{4,12},{5,13},{6,14},{7,15},{8,0},{9,1},... | collective-permute-start | bytes 392 | tf_op jit(solution)/shard_map/ppermute | solution.py:20
  342.0 4.0 %collective-permute-done.27 = f32[2,16]{1,0:T(2,128)S(1)} collective-permute-done((f32[2,16]{1,0:T(2,128)S(1)}, f32[2,16]{1,0:T(2,128)S(1)}, u32[]{:S(2)}, u32[]{:S(2)}) %collective-permute-start.27) | collective-permute-done | bytes 160 | tf_op jit(solution)/shard_map/ppermute | solution.py:20
  346.7 3.0 collective-permute-done.28
  350.4 2.3 copy.49
  (132 shorter events, 56.2 us)
Async XLA Ops:
  7.2 87.4 %all-gather.7.cloned.1.call-start = ((), (), s32[]{:S(2)}) async-start(), calls=%async_computation.6 | async-start | bytes 3145728 | tf_op jit(solution)/shard_map/all_gather | solution.py:122
  7.9 92.1 %all-gather.11.cloned.1.call-start = ((), (), s32[]{:S(2)}) async-start(), calls=%async_computation.8 | async-start | bytes 3145728 | tf_op jit(solution)/shard_map/all_gather | solution.py:124
  8.6 106.1 %all-gather.9.cloned.1.call-start = ((), (), s32[]{:S(2)}) async-start(), calls=%async_computation.7 | async-start | bytes 3145728 | tf_op jit(solution)/shard_map/all_gather | solution.py:123
  15.5 10.6 %collective-permute-start = (bf16[80,2176]{1,0:T(8,128)(2,1)S(1)}, bf16[80,2176]{1,0:T(8,128)(2,1)S(1)}, u32[]{:S(2)}, u32[]{:S(2)}) collective-permute-start(bf16[80,2176]{1,0:T(8,128)(2,1)S(1)} %get-tuple-element.16), channel_id=1, source_target_pairs={{0,1},{1,2},{2,3},{3,4},{4,5},{5,6},{6,7},{7,8},{8,9},{9,10},{10,1... | collective-permute-start | bytes 1044488 | tf_op jit(solution)/shard_map/ppermute | solution.py:106
  16.0 10.6 %collective-permute-start.1 = (bf16[80,2176]{1,0:T(8,128)(2,1)S(1)}, bf16[80,2176]{1,0:T(8,128)(2,1)S(1)}, u32[]{:S(2)}, u32[]{:S(2)}) collective-permute-start(bf16[80,2176]{1,0:T(8,128)(2,1)S(1)} %get-tuple-element.16), channel_id=1, source_target_pairs={{0,15},{1,0},{2,1},{3,2},{4,3},{5,4},{6,5},{7,6},{8,7},{9,8},{10,9... | collective-permute-start | bytes 1044488 | tf_op jit(solution)/shard_map/ppermute | solution.py:113
  26.1 9.5 %collective-permute-start.2 = (bf16[80,2176]{1,0:T(8,128)(2,1)S(1)}, bf16[80,2176]{1,0:T(8,128)(2,1)S(1)}, u32[]{:S(2)}, u32[]{:S(2)}) collective-permute-start(bf16[80,2176]{1,0:T(8,128)(2,1)S(1)} %collective-permute-done), channel_id=1, source_target_pairs={{0,1},{1,2},{2,3},{3,4},{4,5},{5,6},{6,7},{7,8},{8,9},{9,10},{10,1... | collective-permute-start | bytes 1044488 | tf_op jit(solution)/shard_map/ppermute | solution.py:106
  26.6 10.4 %collective-permute-start.3 = (bf16[80,2176]{1,0:T(8,128)(2,1)S(1)}, bf16[80,2176]{1,0:T(8,128)(2,1)S(1)}, u32[]{:S(2)}, u32[]{:S(2)}) collective-permute-start(bf16[80,2176]{1,0:T(8,128)(2,1)S(1)} %collective-permute-done.1), channel_id=1, source_target_pairs={{0,15},{1,0},{2,1},{3,2},{4,3},{5,4},{6,5},{7,6},{8,7},{9,8},{10,9... | collective-permute-start | bytes 1044488 | tf_op jit(solution)/shard_map/ppermute | solution.py:113
  35.6 9.5 %collective-permute-start.4 = (bf16[80,2176]{1,0:T(8,128)(2,1)S(1)}, bf16[80,2176]{1,0:T(8,128)(2,1)S(1)}, u32[]{:S(2)}, u32[]{:S(2)}) collective-permute-start(bf16[80,2176]{1,0:T(8,128)(2,1)S(1)} %collective-permute-done.2), channel_id=1, source_target_pairs={{0,1},{1,2},{2,3},{3,4},{4,5},{5,6},{6,7},{7,8},{8,9},{9,10},{10,1... | collective-permute-start | bytes 1044488 | tf_op jit(solution)/shard_map/ppermute | solution.py:106
  37.0 9.7 %collective-permute-start.5 = (bf16[80,2176]{1,0:T(8,128)(2,1)S(1)}, bf16[80,2176]{1,0:T(8,128)(2,1)S(1)}, u32[]{:S(2)}, u32[]{:S(2)}) collective-permute-start(bf16[80,2176]{1,0:T(8,128)(2,1)S(1)} %collective-permute-done.3), channel_id=1, source_target_pairs={{0,15},{1,0},{2,1},{3,2},{4,3},{5,4},{6,5},{7,6},{8,7},{9,8},{10,9... | collective-permute-start | bytes 1044488 | tf_op jit(solution)/shard_map/ppermute | solution.py:113
  45.1 9.5 %collective-permute-start.6 = (bf16[80,2176]{1,0:T(8,128)(2,1)S(1)}, bf16[80,2176]{1,0:T(8,128)(2,1)S(1)}, u32[]{:S(2)}, u32[]{:S(2)}) collective-permute-start(bf16[80,2176]{1,0:T(8,128)(2,1)S(1)} %collective-permute-done.4), channel_id=1, source_target_pairs={{0,1},{1,2},{2,3},{3,4},{4,5},{5,6},{6,7},{7,8},{8,9},{9,10},{10,1... | collective-permute-start | bytes 1044488 | tf_op jit(solution)/shard_map/ppermute | solution.py:106
  46.7 9.7 %collective-permute-start.7 = (bf16[80,2176]{1,0:T(8,128)(2,1)S(1)}, bf16[80,2176]{1,0:T(8,128)(2,1)S(1)}, u32[]{:S(2)}, u32[]{:S(2)}) collective-permute-start(bf16[80,2176]{1,0:T(8,128)(2,1)S(1)} %collective-permute-done.5), channel_id=1, source_target_pairs={{0,15},{1,0},{2,1},{3,2},{4,3},{5,4},{6,5},{7,6},{8,7},{9,8},{10,9... | collective-permute-start | bytes 1044488 | tf_op jit(solution)/shard_map/ppermute | solution.py:113
  54.6 9.5 %collective-permute-start.8 = (bf16[80,2176]{1,0:T(8,128)(2,1)S(1)}, bf16[80,2176]{1,0:T(8,128)(2,1)S(1)}, u32[]{:S(2)}, u32[]{:S(2)}) collective-permute-start(bf16[80,2176]{1,0:T(8,128)(2,1)S(1)} %collective-permute-done.6), channel_id=1, source_target_pairs={{0,1},{1,2},{2,3},{3,4},{4,5},{5,6},{6,7},{7,8},{8,9},{9,10},{10,1... | collective-permute-start | bytes 1044488 | tf_op jit(solution)/shard_map/ppermute | solution.py:106
  56.4 9.7 %collective-permute-start.9 = (bf16[80,2176]{1,0:T(8,128)(2,1)S(1)}, bf16[80,2176]{1,0:T(8,128)(2,1)S(1)}, u32[]{:S(2)}, u32[]{:S(2)}) collective-permute-start(bf16[80,2176]{1,0:T(8,128)(2,1)S(1)} %collective-permute-done.7), channel_id=1, source_target_pairs={{0,15},{1,0},{2,1},{3,2},{4,3},{5,4},{6,5},{7,6},{8,7},{9,8},{10,9... | collective-permute-start | bytes 1044488 | tf_op jit(solution)/shard_map/ppermute | solution.py:113
  64.2 9.5 %collective-permute-start.10 = (bf16[80,2176]{1,0:T(8,128)(2,1)S(1)}, bf16[80,2176]{1,0:T(8,128)(2,1)S(1)}, u32[]{:S(2)}, u32[]{:S(2)}) collective-permute-start(bf16[80,2176]{1,0:T(8,128)(2,1)S(1)} %collective-permute-done.8), channel_id=1, source_target_pairs={{0,1},{1,2},{2,3},{3,4},{4,5},{5,6},{6,7},{7,8},{8,9},{9,10},{10,1... | collective-permute-start | bytes 1044488 | tf_op jit(solution)/shard_map/ppermute | solution.py:106
  66.1 10.4 %collective-permute-start.11 = (bf16[80,2176]{1,0:T(8,128)(2,1)S(1)}, bf16[80,2176]{1,0:T(8,128)(2,1)S(1)}, u32[]{:S(2)}, u32[]{:S(2)}) collective-permute-start(bf16[80,2176]{1,0:T(8,128)(2,1)S(1)} %collective-permute-done.9), channel_id=1, source_target_pairs={{0,15},{1,0},{2,1},{3,2},{4,3},{5,4},{6,5},{7,6},{8,7},{9,8},{10,9... | collective-permute-start | bytes 1044488 | tf_op jit(solution)/shard_map/ppermute | solution.py:113
  73.7 9.5 %collective-permute-start.12 = (bf16[80,2176]{1,0:T(8,128)(2,1)S(1)}, bf16[80,2176]{1,0:T(8,128)(2,1)S(1)}, u32[]{:S(2)}, u32[]{:S(2)}) collective-permute-start(bf16[80,2176]{1,0:T(8,128)(2,1)S(1)} %collective-permute-done.10), channel_id=1, source_target_pairs={{0,1},{1,2},{2,3},{3,4},{4,5},{5,6},{6,7},{7,8},{8,9},{9,10},{10,1... | collective-permute-start | bytes 1044488 | tf_op jit(solution)/shard_map/ppermute | solution.py:106
  76.5 11.2 %collective-permute-start.13 = (bf16[80,2176]{1,0:T(8,128)(2,1)S(1)}, bf16[80,2176]{1,0:T(8,128)(2,1)S(1)}, u32[]{:S(2)}, u32[]{:S(2)}) collective-permute-start(bf16[80,2176]{1,0:T(8,128)(2,1)S(1)} %collective-permute-done.11), channel_id=1, source_target_pairs={{0,15},{1,0},{2,1},{3,2},{4,3},{5,4},{6,5},{7,6},{8,7},{9,8},{10,9... | collective-permute-start | bytes 1044488 | tf_op jit(solution)/shard_map/ppermute | solution.py:113
  83.2 9.4 %collective-permute-start.14 = (bf16[80,2176]{1,0:T(8,128)(2,1)S(1)}, bf16[80,2176]{1,0:T(8,128)(2,1)S(1)}, u32[]{:S(2)}, u32[]{:S(2)}) collective-permute-start(bf16[80,2176]{1,0:T(8,128)(2,1)S(1)} %collective-permute-done.12), channel_id=1, source_target_pairs={{0,1},{1,2},{2,3},{3,4},{4,5},{5,6},{6,7},{7,8},{8,9},{9,10},{10,1... | collective-permute-start | bytes 1044488 | tf_op jit(solution)/shard_map/ppermute | solution.py:106
  126.2 4.5 %copy-start.2 = (bf16[1,1024,512]{2,1,0:T(8,128)(2,1)S(1)}, bf16[1,1024,512]{2,1,0:T(8,128)(2,1)}, u32[]{:S(2)}) copy-start(bf16[1,1024,512]{2,1,0:T(8,128)(2,1)} %param.19) | copy-start | bytes 3145732
  130.7 35.5 %collective-permute-start.15 = (bf16[8,80,2048]{2,1,0:T(8,128)(2,1)}, bf16[8,80,2048]{2,1,0:T(8,128)(2,1)}, u32[]{:S(2)}, u32[]{:S(2)}) collective-permute-start(bf16[8,80,2048]{2,1,0:T(8,128)(2,1)} %fusion.4), channel_id=1, source_target_pairs={{0,1},{1,0},{2,3},{3,2},{4,5},{5,4},{6,7},{7,6},{8,9},{9,8},{10,11... | collective-permute-start | bytes 7864328 | tf_op jit(solution)/shard_map/ppermute | solution.py:20
  161.2 28.0 %all-to-all-start.2 = ((bf16[16,64,512]{2,1,0:T(8,128)(2,1)}), bf16[16,64,512]{2,1,0:T(8,128)(2,1)S(1)}, u32[]{:S(2)}, u32[]{:S(2)}) async-start(bf16[16,64,512]{2,1,0:T(8,128)(2,1)} %bitcast.16), calls=%async_computation.2 | async-start | bytes 2097152 | tf_op jit(solution)/shard_map/all_to_all | solution.py:26
  166.2 30.0 %copy-start.9 = (s32[16]{0:T(128)S(1)}, s32[16]{0:T(128)}, u32[]{:S(2)}) copy-start(s32[16]{0:T(128)} %param.23) | copy-start | bytes 196
  166.2 30.0 %copy-start.8 = (s32[16]{0:T(128)S(1)}, s32[16]{0:T(128)}, u32[]{:S(2)}) copy-start(s32[16]{0:T(128)} %param.22) | copy-start | bytes 196
  170.4 2.3 copy-start
  172.9 43.6 %collective-permute-start.16 = (bf16[4,80,2048]{2,1,0:T(8,128)(2,1)S(1)}, bf16[4,80,2048]{2,1,0:T(8,128)(2,1)}, u32[]{:S(2)}, u32[]{:S(2)}) collective-permute-start(bf16[4,80,2048]{2,1,0:T(8,128)(2,1)S(1)} %fusion.12), channel_id=1, source_target_pairs={{0,2},{1,3},{2,0},{3,1},{4,6},{5,7},{6,4},{7,5},{8,10},{9,11},{10,... | collective-permute-start | bytes 3932168 | tf_op jit(solution)/shard_map/ppermute | solution.py:20
  189.2 7.1 %copy-start.1 = (bf16[16,64,512]{2,1,0:T(8,128)(2,1)}, bf16[16,64,512]{2,1,0:T(8,128)(2,1)S(1)}, u32[]{:S(2)}) copy-start(bf16[16,64,512]{2,1,0:T(8,128)(2,1)S(1)} %all-to-all-done.2) | copy-start | bytes 3145732
  189.2 43.1 %all-to-all-start.4 = ((bf16[16,16,2048]{2,1,0:T(8,128)(2,1)}), bf16[16,16,2048]{2,1,0:T(8,128)(2,1)}, u32[]{:S(2)}, u32[]{:S(2)}) async-start(bf16[16,16,2048]{2,1,0:T(8,128)(2,1)} %bitcast.18), calls=%async_computation.4 | async-start | bytes 2097152 | tf_op jit(solution)/shard_map/all_to_all | solution.py:26
  219.8 18.1 %collective-permute-start.17 = (bf16[2,80,2048]{2,1,0:T(8,128)(2,1)}, bf16[2,80,2048]{2,1,0:T(8,128)(2,1)}, u32[]{:S(2)}, u32[]{:S(2)}) collective-permute-start(bf16[2,80,2048]{2,1,0:T(8,128)(2,1)} %fusion.22), channel_id=1, source_target_pairs={{0,4},{1,5},{2,6},{3,7},{4,0},{5,1},{6,2},{7,3},{8,12},{9,13},{10,... | collective-permute-start | bytes 1966088 | tf_op jit(solution)/shard_map/ppermute | solution.py:20
  229.1 13.3 %copy-start.7 = (s32[2,1,4]{2,1,0:T(1,128)S(1)}, s32[2,1,4]{2,1,0:T(1,128)}, u32[]{:S(2)}) copy-start(s32[2,1,4]{2,1,0:T(1,128)} %param.24) | copy-start | bytes 100
  229.1 49.8 %copy-start.4 = (bf16[2,40,2048]{2,1,0:T(8,128)(2,1)S(1)}, bf16[2,40,2048]{2,1,0:T(8,128)(2,1)}, u32[]{:S(2)}) copy-start(bf16[2,40,2048]{2,1,0:T(8,128)(2,1)} %param.14) | copy-start | bytes 983044
  232.3 46.7 %all-to-all-start.1 = ((bf16[16,64,512]{2,1,0:T(8,128)(2,1)}), bf16[16,64,512]{2,1,0:T(8,128)(2,1)}, u32[]{:S(2)}, u32[]{:S(2)}) async-start(bf16[16,64,512]{2,1,0:T(8,128)(2,1)} %get-tuple-element.24), calls=%async_computation.1 | async-start | bytes 2097152 | tf_op jit(solution)/shard_map/all_to_all | solution.py:28
  239.2 1.1 copy-start.3
  240.3 37.4 %collective-permute-start.18 = (bf16[1,80,2048]{2,1,0:T(8,128)(2,1)S(1)}, bf16[1,80,2048]{2,1,0:T(8,128)(2,1)S(1)}, u32[]{:S(2)}, u32[]{:S(2)}) collective-permute-start(bf16[1,80,2048]{2,1,0:T(8,128)(2,1)S(1)} %dynamic-slice_convert_fusion.2), channel_id=1, source_target_pairs={{0,8},{1,9},{2,10},{3,11},{4,12},{5,13},{6,14},{7,15},{8,0},{9,1},... | collective-permute-start | bytes 983048 | tf_op jit(solution)/shard_map/ppermute | solution.py:20
  278.9 40.5 %copy-start.6 = (f32[2048]{0:T(1024)S(1)}, f32[2048]{0:T(1024)}, u32[]{:S(2)}) copy-start(f32[2048]{0:T(1024)} %param.18) | copy-start | bytes 24580
  279.0 44.3 %copy-start.5 = (bf16[2,40,2048]{2,1,0:T(8,128)(2,1)}, bf16[2,40,2048]{2,1,0:T(8,128)(2,1)S(1)}, u32[]{:S(2)}) copy-start(bf16[2,40,2048]{2,1,0:T(8,128)(2,1)S(1)} %fusion.21) | copy-start | bytes 983044
  279.0 36.6 %all-to-all-start.3 = ((bf16[16,64,512]{2,1,0:T(8,128)(2,1)}), bf16[16,64,512]{2,1,0:T(8,128)(2,1)S(1)}, u32[]{:S(2)}, u32[]{:S(2)}) async-start(bf16[16,64,512]{2,1,0:T(8,128)(2,1)} %get-tuple-element.23), calls=%async_computation.3 | async-start | bytes 2097152 | tf_op jit(solution)/shard_map/all_to_all | solution.py:28
  283.1 1.3 collective-permute-start.19
  284.4 7.6 %collective-permute-start.20 = (bf16[2,4,2048]{2,1,0:T(4,128)(2,1)S(1)}, bf16[2,4,2048]{2,1,0:T(4,128)(2,1)S(1)}, u32[]{:S(2)}, u32[]{:S(2)}) collective-permute-start(bf16[2,4,2048]{2,1,0:T(4,128)(2,1)S(1)} %add.360), channel_id=1, source_target_pairs={{0,2},{1,3},{2,0},{3,1},{4,6},{5,7},{6,4},{7,5},{8,10},{9,11},{10,... | collective-permute-start | bytes 98312 | tf_op jit(solution)/shard_map/ppermute | solution.py:20
  292.0 9.4 %collective-permute-start.21 = (bf16[2,4,2048]{2,1,0:T(4,128)(2,1)S(1)}, bf16[2,4,2048]{2,1,0:T(4,128)(2,1)S(1)}, u32[]{:S(2)}, u32[]{:S(2)}) collective-permute-start(bf16[2,4,2048]{2,1,0:T(4,128)(2,1)S(1)} %add.361), channel_id=1, source_target_pairs={{0,4},{1,5},{2,6},{3,7},{4,0},{5,1},{6,2},{7,3},{8,12},{9,13},{10,... | collective-permute-start | bytes 98312 | tf_op jit(solution)/shard_map/ppermute | solution.py:20
  301.5 9.2 %collective-permute-start.22 = (bf16[2,4,2048]{2,1,0:T(4,128)(2,1)S(1)}, bf16[2,4,2048]{2,1,0:T(4,128)(2,1)S(1)}, u32[]{:S(2)}, u32[]{:S(2)}) collective-permute-start(bf16[2,4,2048]{2,1,0:T(4,128)(2,1)S(1)} %add.362), channel_id=1, source_target_pairs={{0,8},{1,9},{2,10},{3,11},{4,12},{5,13},{6,14},{7,15},{8,0},{9,1},... | collective-permute-start | bytes 98312 | tf_op jit(solution)/shard_map/ppermute | solution.py:20
  310.9 4.3 %collective-permute-start.23 = (bf16[2,2,4,2048]{3,2,1,0:T(4,128)(2,1)S(1)}, bf16[2,2,4,2048]{3,2,1,0:T(4,128)(2,1)S(1)}, u32[]{:S(2)}, u32[]{:S(2)}) collective-permute-start(bf16[2,2,4,2048]{3,2,1,0:T(4,128)(2,1)S(1)} %broadcast_select_fusion.3), channel_id=1, source_target_pairs={{0,16},{16,0},{1,17},{17,1},{2,18},{18,2},{3,19},{19,3},{4,20},{20... | collective-permute-start | bytes 196616 | tf_op jit(solution)/shard_map/ppermute | solution.py:20
  315.7 31.0 %all-to-all-start.5 = ((bf16[16,16,2048]{2,1,0:T(8,128)(2,1)}), bf16[16,16,2048]{2,1,0:T(8,128)(2,1)S(1)}, u32[]{:S(2)}, u32[]{:S(2)}) async-start(bf16[16,16,2048]{2,1,0:T(8,128)(2,1)} %broadcast_select_fusion.2), calls=%async_computation.5 | async-start | bytes 2097152 | tf_op jit(solution)/shard_map/all_to_all | solution.py:28
  323.5 1.3 collective-permute-start.24
  324.8 3.6 %collective-permute-start.25 = (f32[2,16]{1,0:T(2,128)S(1)}, f32[2,16]{1,0:T(2,128)S(1)}, u32[]{:S(2)}, u32[]{:S(2)}) collective-permute-start(f32[2,16]{1,0:T(2,128)S(1)} %pad_maximum_fusion.2), channel_id=1, source_target_pairs={{0,2},{1,3},{2,0},{3,1},{4,6},{5,7},{6,4},{7,5},{8,10},{9,11},{10,... | collective-permute-start | bytes 392 | tf_op jit(solution)/shard_map/ppermute | solution.py:20
  328.5 9.1 %collective-permute-start.26 = (f32[2,16]{1,0:T(2,128)S(1)}, f32[2,16]{1,0:T(2,128)S(1)}, u32[]{:S(2)}, u32[]{:S(2)}) collective-permute-start(f32[2,16]{1,0:T(2,128)S(1)} %pad_maximum_fusion.3), channel_id=1, source_target_pairs={{0,4},{1,5},{2,6},{3,7},{4,0},{5,1},{6,2},{7,3},{8,12},{9,13},{10,... | collective-permute-start | bytes 392 | tf_op jit(solution)/shard_map/ppermute | solution.py:20
  337.6 8.4 %collective-permute-start.27 = (f32[2,16]{1,0:T(2,128)S(1)}, f32[2,16]{1,0:T(2,128)S(1)}, u32[]{:S(2)}, u32[]{:S(2)}) collective-permute-start(f32[2,16]{1,0:T(2,128)S(1)} %pad_maximum_fusion.4), channel_id=1, source_target_pairs={{0,8},{1,9},{2,10},{3,11},{4,12},{5,13},{6,14},{7,15},{8,0},{9,1},... | collective-permute-start | bytes 392 | tf_op jit(solution)/shard_map/ppermute | solution.py:20
  346.0 3.6 %collective-permute-start.28 = (f32[2,16]{1,0:T(2,128)S(1)}, f32[2,16]{1,0:T(2,128)S(1)}, u32[]{:S(2)}, u32[]{:S(2)}) collective-permute-start(f32[2,16]{1,0:T(2,128)S(1)} %pad_maximum_fusion.5), channel_id=1, source_target_pairs={{0,16},{16,0},{1,17},{17,1},{2,18},{18,2},{3,19},{19,3},{4,20},{20... | collective-permute-start | bytes 392 | tf_op jit(solution)/shard_map/ppermute | solution.py:20
Sparse Core Ops, SparseCore 0:
  9.5 35.7 all-gather.6
  46.9 33.1 all-gather.10
  81.6 33.1 all-gather.8
